TPU v7x, 512 devices: a whole 4x4x16 slice. The times are simulated.
512 devices in a mesh: seq: 128 (over z, x, core), head: 4 (over y).
Axes of the slice: x: 4, y: 4, z: 16, core: 2. Of those that a mesh axis runs over, the one named last changes fastest.
Arguments:
- queries: bfloat16 [32768, 512], P('seq', 'head'), may hold values from -16 to 16
- keys: bfloat16 [32768, 512], P('seq', 'head'), may hold values from -16 to 16
- values: bfloat16 [32768, 512], P('seq', 'head'), may hold values from -16 to 16
- out_weight: bfloat16 [512, 512], replicated, may hold values from -0.5 to 0.5
Outputs:
- mixed: bfloat16 [32768, 512], P(('seq', 'head'))
All inputs are finite; a program needn't handle non-finite values.
Results may differ from a plain program's by a relative error of at most 0.00185.
The roundings to bfloat16 on the way count: a program that leaves them out, or rounds other values in their place, can miss the bound.
Values may be sent and summed in bfloat16 or wider, within the bound.
A program may use at most 128 MiB of HBM per device.

v0:
```python
import math
import jax
import jax.numpy as jnp
from jax import lax
from jax.sharding import PartitionSpec as P

HD = 64
LEAF = 128


def extended_2(cells, sides, width):
    for axis, dim in sides:
        count = lax.axis_size(axis)
        ends = count - 1
        head = lax.slice_in_dim(cells, 0, width, axis=dim)
        tail = lax.slice_in_dim(cells, cells.shape[dim] - width, cells.shape[dim], axis=dim)
        cells = jnp.concatenate(
            [
                lax.ppermute(tail, axis, [(i, (i + 1) % count) for i in range(ends)]),
                cells,
                lax.ppermute(head, axis, [((i + 1) % count, i) for i in range(ends)]),
            ],
            axis=dim,
        )
    return cells


def as_sent(x):

    def short(part):
        return part.astype(jnp.bfloat16) if part.dtype == jnp.float32 else part

    return jax.tree.map(short, x)


def average_pairs(stacked):
    widened = stacked.astype(jnp.float32).reshape(2, stacked.shape[1] // 2, 2, stacked.shape[2])
    return (0.5 * (widened[:, :, 0] + widened[:, :, 1])).astype(jnp.bfloat16)


def near_set(leaf, extended, seq_index, blocks_dev, seq_size):
    positions = jnp.arange(LEAF, dtype=jnp.int32)
    upper_half = positions >= LEAF // 2
    global_leaf = seq_index * blocks_dev + leaf
    all_blocks = seq_size * blocks_dev
    key_parts = [lax.dynamic_slice_in_dim(extended[0], leaf * LEAF, 3 * LEAF, 1)]
    neighbour = global_leaf - 1 + jnp.arange(3 * LEAF, dtype=jnp.int32) // LEAF
    valid_parts = [(neighbour >= 0) & (neighbour < all_blocks)]
    local_block = leaf >> 1
    global_block = global_leaf >> 1
    parity = global_leaf >> 0 & 1
    level_blocks = all_blocks >> 1
    key_parts.append(lax.dynamic_slice_in_dim(extended[1], local_block * LEAF, LEAF, 1))
    key_parts.append(lax.dynamic_slice_in_dim(extended[1], (local_block + 2) * LEAF, LEAF, 1))
    valid_parts.append((global_block >= 1) & jnp.logical_not(upper_half & (parity == 0)))
    valid_parts.append(
        (global_block + 1 < level_blocks)
        & jnp.logical_not(jnp.logical_not(upper_half) & (parity == 1))
    )
    return (jnp.concatenate(key_parts, axis=1), jnp.concatenate(valid_parts, axis=0))


def shards(queries, keys, values, out_weight):
    tok_count = queries.shape[0]
    width = queries.shape[1]
    seq_size = lax.axis_size("seq")
    seq_index = lax.axis_index("seq")
    blocks_dev = tok_count // LEAF
    near_count = blocks_dev.bit_length() - 1
    far_count = max(0, seq_size.bit_length() - 2)
    scale = 1.0 / math.sqrt(HD)
    positions = jnp.arange(LEAF, dtype=jnp.int32)
    upper_half = positions >= LEAF // 2
    local = [jnp.stack([keys, values], axis=0)]
    local.append(average_pairs(local[-1]))
    extended = [extended_2(stacked, (("seq", 1),), LEAF) for stacked in local]
    own_block = local[near_count]
    far_pairs = []
    far_valid = []
    everything = lax.all_gather(own_block, "seq", axis=1, tiled=True)
    for level_far in range(1, far_count + 1):
        everything = average_pairs(everything)
        group = seq_index >> level_far
        padded = jnp.pad(everything, ((0, 0), (LEAF, LEAF), (0, 0)))
        lower = lax.dynamic_slice_in_dim(padded, group * LEAF, LEAF, 1)
        upper = lax.dynamic_slice_in_dim(padded, (group + 2) * LEAF, LEAF, 1)
        far_pairs.append(jnp.concatenate([lower, upper], axis=1))
    for level_far in range(1, far_count + 1):
        group = seq_index >> level_far
        parity = seq_index >> level_far - 1 & 1
        far_valid.append((group >= 1) & jnp.logical_not(upper_half & (parity == 0)))
        far_valid.append(
            (group + 1 < seq_size >> level_far)
            & jnp.logical_not(jnp.logical_not(upper_half) & (parity == 1))
        )
    far_keys = jnp.concatenate(far_pairs, axis=1)
    far_mask = jnp.concatenate(far_valid, axis=0)
    leaves_step = min(blocks_dev, max(1, 512 // LEAF))
    step_count = blocks_dev // leaves_step

    def attend(step):
        leaves = step * leaves_step + jnp.arange(leaves_step, dtype=jnp.int32)
        near_keys, near_mask = jax.vmap(
            lambda leaf: near_set(leaf, extended, seq_index, blocks_dev, seq_size)
        )(leaves)
        query_block = queries.reshape(leaves_step, LEAF, width)
        head_outputs = []
        for head_number in range(width // HD):
            low_col = head_number * HD
            high_col = low_col + HD
            near_scores = (
                jnp.einsum(
                    "nhs,nos->nho",
                    query_block[:, :, low_col:high_col],
                    near_keys[:, 0, :, low_col:high_col],
                    preferred_element_type=jnp.float32,
                )
                * scale
            )
            near_scores = jnp.where(near_mask[:, None, :], near_scores, -jnp.inf)
            peak = jnp.max(near_scores, axis=-1, keepdims=True)
            far_scores = (
                jnp.einsum(
                    "qs,os->qo",
                    queries[:, low_col:high_col],
                    far_keys[0, :, low_col:high_col],
                    preferred_element_type=jnp.float32,
                )
                * scale
            )
            far_scores = far_scores.reshape(leaves_step, LEAF, far_scores.shape[-1])
            far_scores = jnp.where(far_mask[None, None, :], far_scores, -jnp.inf)
            peak = jnp.maximum(peak, jnp.max(far_scores, axis=-1, keepdims=True))
            near_weights = jnp.exp(near_scores - peak)
            total = jnp.sum(near_weights, axis=-1)
            numer = jnp.einsum(
                "fkm,fmp->fkp",
                near_weights.astype(jnp.bfloat16),
                near_keys[:, 1, :, low_col:high_col],
                preferred_element_type=jnp.float32,
            )
            far_weights = jnp.exp(far_scores - peak)
            total = total + jnp.sum(far_weights, axis=-1)
            far_rounded = far_weights.astype(jnp.bfloat16).reshape(
                leaves_step * LEAF, far_weights.shape[-1]
            )
            far_numer = jnp.dot(
                far_rounded, far_keys[1, :, low_col:high_col], preferred_element_type=jnp.float32
            )
            numer = numer + far_numer.reshape(leaves_step, LEAF, HD)
            head_outputs.append((numer / total[..., None]).astype(jnp.bfloat16))
        return jnp.concatenate(head_outputs, axis=-1).reshape(leaves_step * LEAF, width)

    attended = lax.map(attend, jnp.arange(step_count, dtype=jnp.int32)).reshape(tok_count, width)
    gathered_rows = lax.all_to_all(
        as_sent(attended), "head", split_axis=0, concat_axis=1, tiled=True
    ).astype(attended.dtype)
    return jnp.dot(gathered_rows, out_weight, preferred_element_type=jnp.float32).astype(
        jnp.bfloat16
    )


def solution(mesh):
    in_specs = (P("seq", "head"), P("seq", "head"), P("seq", "head"), P())
    out_specs = P(("seq", "head"), None)
    return jax.shard_map(shards, mesh=mesh, in_specs=in_specs, out_specs=out_specs, check_vma=False)
```

profile of v0, /device:TPU:32, one launch (start us, length us, event | category | flops | bytes accessed | tf_op | source)
XLA Modules:
  0.0 354.0 jit_solution(11749175016474953703)
XLA Ops:
  11.6 5.8 %collective-permute-start.3 = (bf16[2,128,128]{2,0,1:T(2,128)(2,1)S(1)}, bf16[2,128,128]{2,0,1:T(2,128)(2,1)S(1)}, u32[]{:S(2)}, u32[]{:S(2)}) collective-permute-start(bf16[2,128,128]{2,0,1:T(2,128)(2,1)S(1)} %fusion.76), channel_id=1, source_target_pairs={{4,0},{8,4},{12,8},{16,12},{20,16},{24,20},{28,24},{32,28},{36,32}... | collective-permute-start | bytes 196616 | tf_op jit(solution)/shard_map/ppermute | solution.py:21
  21.4 5.8 %collective-permute-start.1 = (bf16[2,128,128]{2,0,1:T(2,128)(2,1)S(1)}, bf16[2,128,128]{2,0,1:T(2,128)(2,1)S(1)}, u32[]{:S(2)}, u32[]{:S(2)}) collective-permute-start(bf16[2,128,128]{2,0,1:T(2,128)(2,1)S(1)} %get-tuple-element.46), channel_id=1, source_target_pairs={{4,0},{8,4},{12,8},{16,12},{20,16},{24,20},{28,24},{32,28},{36,32}... | collective-permute-start | bytes 196616 | tf_op jit(solution)/shard_map/ppermute | solution.py:21
  37.7 124.1 %all-gather.3.cloned.1.call-done = bf16[2,16384,1,128]{3,0,2,1:T(2,128)(2,1)} async-done(((bf16[2,128,1,128]{3,0,2,1:T(2,128)(2,1)}), bf16[2,16384,1,128]{3,0,2,1:T(2,128)(2,1)}) %all-gather.3.cloned.1.call-update) | async-done | bytes 8388624 | tf_op jit(solution)/shard_map/all_gather | solution.py:80
  161.8 5.1 %copy.50 = bf16[2,16384,1,128]{3,1,0,2:T(8,128)(2,1)S(1)} copy(bf16[2,16384,1,128]{3,0,2,1:T(2,128)(2,1)} %all-gather.3.cloned.1.call-done) | data formatting | bytes 16777216 | tf_op jit(solution)/shard_map/all_gather | solution.py:80
  166.8 13.0 %fusion.63 = (f32[2,8192,1,128]{3,2,1,0:T(1,128)}, f32[2,8192,1,128]{3,2,1,0:T(1,128)}) fusion(bf16[2,8192,2,128]{3,2,1,0:T(2,128)(2,1)S(1)} %bitcast.97), kind=kLoop, calls=%fused_computation.146 | loop fusion | bytes 33554432 | tf_op jit(solution)/shard_map/slice | solution.py:38
  179.8 18.0 %copy.76 = f32[2,8192,1,128]{1,3,0,2:T(8,128)} copy(f32[2,8192,1,128]{3,2,1,0:T(1,128)} %get-tuple-element.22) | data formatting | bytes 16777216
  197.8 18.0 %copy.77 = f32[2,8192,1,128]{1,3,0,2:T(8,128)} copy(f32[2,8192,1,128]{3,2,1,0:T(1,128)} %get-tuple-element.21) | data formatting | bytes 16777216
  215.8 9.4 %multiply_convert_fusion = bf16[2,8192,1,128]{1,3,0,2:T(8,128)(2,1)} fusion(f32[2,8192,1,128]{1,3,0,2:T(8,128)} %copy.76, f32[2,8192,1,128]{1,3,0,2:T(8,128)} %copy.77), kind=kLoop, calls=%fused_computation.3 | loop fusion | flops 6291456 | bytes 20971520 | tf_op jit(solution)/shard_map/convert_element_type | solution.py:38
  225.2 7.0 %copy.53 = f32[2,8192,1,128]{3,1,0,2:T(8,128)} copy(bf16[2,8192,1,128]{1,3,0,2:T(8,128)(2,1)} %multiply_convert_fusion) | data formatting | bytes 12582912 | tf_op jit(solution)/shard_map/convert_element_type | solution.py:37
  232.3 11.5 %fusion.62 = (f32[2,4096,1,128]{3,2,1,0:T(1,128)}, f32[2,4096,1,128]{3,2,1,0:T(1,128)}) fusion(f32[2,4096,2,128]{3,2,1,0:T(2,128)} %bitcast.102), kind=kLoop, calls=%fused_computation.145 | loop fusion | bytes 16777216 | tf_op jit(solution)/shard_map/slice | solution.py:38
  243.8 10.2 %copy.78 = f32[2,4096,1,128]{1,3,0,2:T(8,128)} copy(f32[2,4096,1,128]{3,2,1,0:T(1,128)} %get-tuple-element.20) | data formatting | bytes 8388608
  254.0 10.2 %copy.79 = f32[2,4096,1,128]{1,3,0,2:T(8,128)} copy(f32[2,4096,1,128]{3,2,1,0:T(1,128)} %get-tuple-element.19) | data formatting | bytes 8388608
  264.1 4.3 %multiply_convert_fusion.1 = bf16[2,4096,1,128]{1,3,0,2:T(8,128)(2,1)S(1)} fusion(f32[2,4096,1,128]{1,3,0,2:T(8,128)} %copy.78, f32[2,4096,1,128]{1,3,0,2:T(8,128)} %copy.79), kind=kLoop, calls=%fused_computation.4 | loop fusion | flops 3145728 | bytes 10485760 | tf_op jit(solution)/shard_map/convert_element_type | solution.py:38
  268.5 2.9 copy.56
  271.4 7.9 %fusion.64 = (f32[2,2048,1,128]{3,2,1,0:T(1,128)}, f32[2,2048,1,128]{3,2,1,0:T(1,128)}) fusion(f32[2,2048,2,128]{3,2,1,0:T(2,128)} %bitcast.105), kind=kLoop, calls=%fused_computation.147 | loop fusion | bytes 8388608 | tf_op jit(solution)/shard_map/slice | solution.py:38
  279.3 6.1 %copy.80 = f32[2,2048,1,128]{1,3,0,2:T(8,128)} copy(f32[2,2048,1,128]{3,2,1,0:T(1,128)} %get-tuple-element.32) | data formatting | bytes 4194304
  285.4 6.1 %copy.81 = f32[2,2048,1,128]{1,3,0,2:T(8,128)} copy(f32[2,2048,1,128]{3,2,1,0:T(1,128)} %get-tuple-element.23) | data formatting | bytes 4194304
  291.5 3.6 %multiply_convert_fusion.2 = bf16[2,2048,1,128]{1,3,0,2:T(8,128)(2,1)} fusion(f32[2,2048,1,128]{1,3,0,2:T(8,128)} %copy.80, f32[2,2048,1,128]{1,3,0,2:T(8,128)} %copy.81), kind=kLoop, calls=%fused_computation.11 | loop fusion | flops 1572864 | bytes 5242880 | tf_op jit(solution)/shard_map/convert_element_type | solution.py:38
  295.1 2.6 copy.59
  297.7 5.4 %fusion.65 = (f32[2,1024,1,128]{3,2,1,0:T(1,128)}, f32[2,1024,1,128]{3,2,1,0:T(1,128)}) fusion(f32[2,1024,2,128]{3,2,1,0:T(2,128)} %bitcast.108), kind=kLoop, calls=%fused_computation.148 | loop fusion | bytes 4194304 | tf_op jit(solution)/shard_map/slice | solution.py:38
  303.1 3.6 %copy.82 = f32[2,1024,1,128]{1,3,0,2:T(8,128)} copy(f32[2,1024,1,128]{3,2,1,0:T(1,128)} %get-tuple-element.36) | data formatting | bytes 2097152
  306.7 3.6 %copy.83 = f32[2,1024,1,128]{1,3,0,2:T(8,128)} copy(f32[2,1024,1,128]{3,2,1,0:T(1,128)} %get-tuple-element.34) | data formatting | bytes 2097152
  313.3 3.5 fusion.66
  336.6 9.7 %all_to_all.19 = bf16[4,64,128]{2,1,0:T(8,128)(2,1)S(1)} all-to-all(bf16[4,64,128]{2,1,0:T(8,128)(2,1)S(1)} %bitcast.121), channel_id=1, replica_groups=mesh['seq'=128,'head'=4] {'head'}, dimensions={0} | all-to-all | bytes 131072 | tf_op jit(solution)/shard_map/all_to_all | solution.py:155
  (125 shorter events, 42.7 us)
Async XLA Ops:
  6.5 339.8 %copy-start = (bf16[512,512]{1,0:T(8,128)(2,1)S(1)}, bf16[512,512]{1,0:T(8,128)(2,1)}, u32[]{:S(2)}) copy-start(bf16[512,512]{1,0:T(8,128)(2,1)} %param.7) | copy-start | bytes 1572868
  6.5 155.2 %all-gather.3.cloned.1.call-start = ((), (), s32[]{:S(2)}) async-start(), calls=%async_computation.1 | async-start | bytes 8454144 | tf_op jit(solution)/shard_map/all_gather | solution.py:80
  9.6 21.1 %collective-permute-start.2 = (bf16[2,128,128]{2,0,1:T(2,128)(2,1)S(1)}, bf16[2,128,128]{2,0,1:T(2,128)(2,1)S(1)}, u32[]{:S(2)}, u32[]{:S(2)}) collective-permute-start(bf16[2,128,128]{2,0,1:T(2,128)(2,1)S(1)} %fusion.76), channel_id=1, source_target_pairs={{0,4},{4,8},{8,12},{12,16},{16,20},{20,24},{24,28},{28,32},{32,36}... | collective-permute-start | bytes 196616 | tf_op jit(solution)/shard_map/ppermute | solution.py:19
  11.6 19.1 %collective-permute-start.3 = (bf16[2,128,128]{2,0,1:T(2,128)(2,1)S(1)}, bf16[2,128,128]{2,0,1:T(2,128)(2,1)S(1)}, u32[]{:S(2)}, u32[]{:S(2)}) collective-permute-start(bf16[2,128,128]{2,0,1:T(2,128)(2,1)S(1)} %fusion.76), channel_id=1, source_target_pairs={{4,0},{8,4},{12,8},{16,12},{20,16},{24,20},{28,24},{32,28},{36,32}... | collective-permute-start | bytes 196616 | tf_op jit(solution)/shard_map/ppermute | solution.py:21
  19.5 13.4 %collective-permute-start = (bf16[2,128,128]{2,0,1:T(2,128)(2,1)S(1)}, bf16[2,128,128]{2,0,1:T(2,128)(2,1)S(1)}, u32[]{:S(2)}, u32[]{:S(2)}) collective-permute-start(bf16[2,128,128]{2,0,1:T(2,128)(2,1)S(1)} %get-tuple-element.45), channel_id=1, source_target_pairs={{0,4},{4,8},{8,12},{12,16},{16,20},{20,24},{24,28},{28,32},{32,36}... | collective-permute-start | bytes 196616 | tf_op jit(solution)/shard_map/ppermute | solution.py:19
  21.4 11.5 %collective-permute-start.1 = (bf16[2,128,128]{2,0,1:T(2,128)(2,1)S(1)}, bf16[2,128,128]{2,0,1:T(2,128)(2,1)S(1)}, u32[]{:S(2)}, u32[]{:S(2)}) collective-permute-start(bf16[2,128,128]{2,0,1:T(2,128)(2,1)S(1)} %get-tuple-element.46), channel_id=1, source_target_pairs={{4,0},{8,4},{12,8},{16,12},{20,16},{24,20},{28,24},{32,28},{36,32}... | collective-permute-start | bytes 196616 | tf_op jit(solution)/shard_map/ppermute | solution.py:21
  32.0 3.3 copy-start.9
  35.2 1.2 copy-start.5
  328.9 2.2 copy-start.1
  331.2 1.2 copy-start.2
  331.3 1.4 copy-start.7
  331.3 1.4 copy-start.8
  332.5 1.1 copy-start.4
  332.6 1.2 copy-start.6
  333.3 1.3 copy-start.3
Sparse Core Ops, SparseCore 0:
  10.5 151.2 all-gather.2
where the time goes:
time: 357 us; the launch traced here: 354 us
  local copies, waits for them, and re-layouts  161 us (45%)
  waiting for transfers between devices  124 us (35%)
  other arithmetic  24 us (7%)
  starting transfers between devices  15.3 us (4%)
  between operations  14 us (4%)
  blocking collectives  9.71 us (3%)
  matrix products  5.36 us (2%)
    all_gather x1, waiting for transfers between devices, shards(): everything = lax.all_gather(own_block, 'seq', axis=1, tiled=True)  124 us
    unnamed x54, local copies, waits for them, and re-layouts  90 us
    slice x6, local copies, waits for them, and re-layouts, average_pairs(): return (0.5 * (widened[:, :, 0] + widened[:, :, 1])).astype(jnp.bfloat16)  43.9 us
    convert_element_type x8, other arithmetic, average_pairs(): return (0.5 * (widened[:, :, 0] + widened[:, :, 1])).astype(jnp.bfloat16)  21.3 us
    convert_element_type x5, local copies, waits for them, and re-layouts, average_pairs(): stacked.astype(jnp.float32)  14.7 us
    ppermute x2, starting transfers between devices, extended_2(): lax.ppermute(head, axis, [((i + 1) % count, i) for i in range(ends)])  11.5 us
    all_to_all x1, blocking collectives, shards(): lax.all_to_all(as_sent(attended), 'head', split_axis=0, concat_axis=1, ti...  9.71 us
  transfers between devices with their start and end apart: 5, of which 1 were waited for; matrix products, arithmetic and copies ran while one was open for 4% of the time, Pallas kernels for 0%

commit v1 on v0

--- a/solution.py
+++ b/solution.py
@@ -6,6 +6,11 @@
 
 HD = 64
 LEAF = 128
+
+
+def wait_arrays(field_in, net_axis):
+    plain = lax.all_to_all(jnp.stack(lax.psum(1, net_axis) * [field_in], 0), net_axis, 0, 0)
+    return jnp.concatenate(plain, axis=1)
 
 
 def extended_2(cells, sides, width):
@@ -77,7 +82,7 @@
     own_block = local[near_count]
     far_pairs = []
     far_valid = []
-    everything = lax.all_gather(own_block, "seq", axis=1, tiled=True)
+    everything = wait_arrays(own_block, "seq")
     for level_far in range(1, far_count + 1):
         everything = average_pairs(everything)
         group = seq_index >> level_far

time: 357 us -> 599 us (1.68)
  the two profiles are of different devices: /device:TPU:32 before, /device:TPU:64 now
where the time goes in v1:
time: 599 us; the launch traced here: 596 us
  waiting for transfers between devices  343 us (57%)
  local copies, waits for them, and re-layouts  167 us (28%)
  other arithmetic  35.5 us (6%)
  starting transfers between devices  34.7 us (6%)
  blocking collectives  9.89 us (2%)
    ppermute x2, waiting for transfers between devices, extended_2(): lax.ppermute(tail, axis, [(i, (i + 1) % count) for i in range(ends)])  343 us
    unnamed x54, local copies, waits for them, and re-layouts  90.1 us
    slice x6, local copies, waits for them, and re-layouts, average_pairs(): return (0.5 * (widened[:, :, 0] + widened[:, :, 1])).astype(jnp.bfloat16)  50.6 us
    convert_element_type x7, other arithmetic, average_pairs(): return (0.5 * (widened[:, :, 0] + widened[:, :, 1])).astype(jnp.bfloat16)  21.5 us
    all_to_all x1, starting transfers between devices, wait_arrays(): lax.all_to_all(jnp.stack(lax.psum(1, net_axis) * [field_in], 0), net_axis...  19.1 us
    convert_element_type x5, local copies, waits for them, and re-layouts, average_pairs(): stacked.astype(jnp.float32)  14.7 us
  transfers between devices with their start and end apart: 5, of which 1 were waited for; matrix products, arithmetic and copies ran while one was open for 2% of the time, Pallas kernels for 0%

profile of v1, /device:TPU:64, one launch (start us, length us, event | category | flops | bytes accessed | tf_op | source)
XLA Modules:
  0.0 596.3 jit_solution(8958414069375583554)
XLA Ops:
  2.4 5.4 stack.20
  7.7 19.1 %all-to-all-start = ((bf16[128,2,128,128]{3,2,1,0:T(8,128)(2,1)}), bf16[128,2,128,128]{3,2,1,0:T(8,128)(2,1)}, u32[]{:S(2)}, u32[]{:S(2)}) async-start(bf16[128,2,128,128]{3,2,1,0:T(8,128)(2,1)} %stack.20), calls=%async_computation | async-start | bytes 16777216 | tf_op jit(solution)/shard_map/all_to_all | solution.py:12
  29.0 5.6 collective-permute-start.3
  37.0 5.9 collective-permute-start.1
  46.5 343.2 %collective-permute-done.2 = bf16[2,128,128]{2,0,1:T(2,128)(2,1)S(1)} collective-permute-done((bf16[2,128,128]{2,0,1:T(2,128)(2,1)S(1)}, bf16[2,128,128]{2,0,1:T(2,128)(2,1)S(1)}, u32[]{:S(2)}, u32[]{:S(2)}) %collective-permute-start.2) | collective-permute-done | bytes 65568 | tf_op jit(solution)/shard_map/ppermute | solution.py:24
  396.7 11.2 %copy_convert_fusion = f32[128,2,128,128]{3,2,0,1:T(8,128)} fusion(bf16[128,2,128,128]{3,2,1,0:T(8,128)(2,1)} %all-to-all-done), kind=kLoop, calls=%fused_computation.3 | loop fusion | flops 4194304 | bytes 25165824 | tf_op jit(solution)/shard_map/convert_element_type | solution.py:42
  407.9 19.3 %fusion.63 = (f32[2,8192,1,128]{3,2,1,0:T(1,128)}, f32[2,8192,1,128]{3,2,1,0:T(1,128)}) fusion(f32[2,8192,2,128]{3,2,1,0:T(2,128)} %bitcast.98), kind=kLoop, calls=%fused_computation.147 | loop fusion | bytes 33554432 | tf_op jit(solution)/shard_map/slice | solution.py:43
  427.2 18.0 %copy.77 = f32[2,8192,1,128]{1,3,0,2:T(8,128)} copy(f32[2,8192,1,128]{3,2,1,0:T(1,128)} %get-tuple-element.20) | data formatting | bytes 16777216
  445.2 18.0 %copy.78 = f32[2,8192,1,128]{1,3,0,2:T(8,128)} copy(f32[2,8192,1,128]{3,2,1,0:T(1,128)} %get-tuple-element.19) | data formatting | bytes 16777216
  463.3 9.4 %multiply_convert_fusion = bf16[2,8192,1,128]{1,3,0,2:T(8,128)(2,1)} fusion(f32[2,8192,1,128]{1,3,0,2:T(8,128)} %copy.77, f32[2,8192,1,128]{1,3,0,2:T(8,128)} %copy.78), kind=kLoop, calls=%fused_computation.4 | loop fusion | flops 6291456 | bytes 20971520 | tf_op jit(solution)/shard_map/convert_element_type | solution.py:43
  472.7 7.0 %copy.54 = f32[2,8192,1,128]{3,1,0,2:T(8,128)} copy(bf16[2,8192,1,128]{1,3,0,2:T(8,128)(2,1)} %multiply_convert_fusion) | data formatting | bytes 12582912 | tf_op jit(solution)/shard_map/convert_element_type | solution.py:42
  479.7 11.8 %fusion.64 = (f32[2,4096,1,128]{3,2,1,0:T(1,128)}, f32[2,4096,1,128]{3,2,1,0:T(1,128)}) fusion(f32[2,4096,2,128]{3,2,1,0:T(2,128)} %bitcast.101), kind=kLoop, calls=%fused_computation.148 | loop fusion | bytes 16777216 | tf_op jit(solution)/shard_map/slice | solution.py:43
  491.5 10.1 %copy.79 = f32[2,4096,1,128]{1,3,0,2:T(8,128)} copy(f32[2,4096,1,128]{3,2,1,0:T(1,128)} %get-tuple-element.22) | data formatting | bytes 8388608
  501.7 10.2 %copy.80 = f32[2,4096,1,128]{1,3,0,2:T(8,128)} copy(f32[2,4096,1,128]{3,2,1,0:T(1,128)} %get-tuple-element.21) | data formatting | bytes 8388608
  511.8 4.3 multiply_convert_fusion.1
  519.1 8.0 %fusion.65 = (f32[2,2048,1,128]{3,2,1,0:T(1,128)}, f32[2,2048,1,128]{3,2,1,0:T(1,128)}) fusion(f32[2,2048,2,128]{3,2,1,0:T(2,128)} %bitcast.104), kind=kLoop, calls=%fused_computation.149 | loop fusion | bytes 8388608 | tf_op jit(solution)/shard_map/slice | solution.py:43
  527.1 6.1 %copy.81 = f32[2,2048,1,128]{1,3,0,2:T(8,128)} copy(f32[2,2048,1,128]{3,2,1,0:T(1,128)} %get-tuple-element.32) | data formatting | bytes 4194304
  533.2 6.1 %copy.82 = f32[2,2048,1,128]{1,3,0,2:T(8,128)} copy(f32[2,2048,1,128]{3,2,1,0:T(1,128)} %get-tuple-element.23) | data formatting | bytes 4194304
  539.3 3.6 multiply_convert_fusion.2
  545.5 5.4 fusion.66
  551.0 3.6 copy.83
  554.6 3.6 copy.84
  561.1 3.5 fusion.67
  585.5 9.9 %all_to_all.24 = bf16[4,64,128]{2,1,0:T(8,128)(2,1)S(1)} all-to-all(bf16[4,64,128]{2,1,0:T(8,128)(2,1)S(1)} %bitcast.120), channel_id=1, replica_groups=mesh['seq'=128,'head'=4] {'head'}, dimensions={0} | all-to-all | bytes 131072 | tf_op jit(solution)/shard_map/all_to_all | solution.py:160
  (125 shorter events, 47.1 us)
Async XLA Ops:
  0.0 595.4 %copy-start = (bf16[512,512]{1,0:T(8,128)(2,1)S(1)}, bf16[512,512]{1,0:T(8,128)(2,1)}, u32[]{:S(2)}) copy-start(bf16[512,512]{1,0:T(8,128)(2,1)} %param.7) | copy-start | bytes 1572868
  7.7 26.8 %copy-start.7 = (bf16[256,128]{1,0:T(8,128)(2,1)S(1)}, bf16[256,128]{1,0:T(8,128)(2,1)}, u32[]{:S(2)}) copy-start(bf16[256,128]{1,0:T(8,128)(2,1)} %param.5) | copy-start | bytes 196612
  7.7 27.0 %copy-start.8 = (bf16[256,128]{1,0:T(8,128)(2,1)S(1)}, bf16[256,128]{1,0:T(8,128)(2,1)}, u32[]{:S(2)}) copy-start(bf16[256,128]{1,0:T(8,128)(2,1)} %param.6) | copy-start | bytes 196612
  7.7 388.9 %all-to-all-start = ((bf16[128,2,128,128]{3,2,1,0:T(8,128)(2,1)}), bf16[128,2,128,128]{3,2,1,0:T(8,128)(2,1)}, u32[]{:S(2)}, u32[]{:S(2)}) async-start(bf16[128,2,128,128]{3,2,1,0:T(8,128)(2,1)} %stack.20), calls=%async_computation | async-start | bytes 16777216 | tf_op jit(solution)/shard_map/all_to_all | solution.py:12
  26.9 362.8 %collective-permute-start.2 = (bf16[2,128,128]{2,0,1:T(2,128)(2,1)S(1)}, bf16[2,128,128]{2,0,1:T(2,128)(2,1)S(1)}, u32[]{:S(2)}, u32[]{:S(2)}) collective-permute-start(bf16[2,128,128]{2,0,1:T(2,128)(2,1)S(1)} %fusion.46), channel_id=1, source_target_pairs={{0,4},{4,8},{8,12},{12,16},{16,20},{20,24},{24,28},{28,32},{32,36}... | collective-permute-start | bytes 196616 | tf_op jit(solution)/shard_map/ppermute | solution.py:24
  29.0 360.7 %collective-permute-start.3 = (bf16[2,128,128]{2,0,1:T(2,128)(2,1)S(1)}, bf16[2,128,128]{2,0,1:T(2,128)(2,1)S(1)}, u32[]{:S(2)}, u32[]{:S(2)}) collective-permute-start(bf16[2,128,128]{2,0,1:T(2,128)(2,1)S(1)} %fusion.46), channel_id=1, source_target_pairs={{4,0},{8,4},{12,8},{16,12},{20,16},{24,20},{28,24},{32,28},{36,32}... | collective-permute-start | bytes 196616 | tf_op jit(solution)/shard_map/ppermute | solution.py:26
  35.1 356.8 %collective-permute-start = (bf16[2,128,128]{2,0,1:T(2,128)(2,1)S(1)}, bf16[2,128,128]{2,0,1:T(2,128)(2,1)S(1)}, u32[]{:S(2)}, u32[]{:S(2)}) collective-permute-start(bf16[2,128,128]{2,0,1:T(2,128)(2,1)S(1)} %get-tuple-element.45), channel_id=1, source_target_pairs={{0,4},{4,8},{8,12},{12,16},{16,20},{20,24},{24,28},{28,32},{32,36}... | collective-permute-start | bytes 196616 | tf_op jit(solution)/shard_map/ppermute | solution.py:24
  37.0 354.8 %collective-permute-start.1 = (bf16[2,128,128]{2,0,1:T(2,128)(2,1)S(1)}, bf16[2,128,128]{2,0,1:T(2,128)(2,1)S(1)}, u32[]{:S(2)}, u32[]{:S(2)}) collective-permute-start(bf16[2,128,128]{2,0,1:T(2,128)(2,1)S(1)} %get-tuple-element.46), channel_id=1, source_target_pairs={{4,0},{8,4},{12,8},{16,12},{20,16},{24,20},{28,24},{32,28},{36,32}... | collective-permute-start | bytes 196616 | tf_op jit(solution)/shard_map/ppermute | solution.py:26
  390.9 3.3 copy-start.9
  394.2 1.2 copy-start.5
  577.9 2.2 copy-start.1
  580.2 1.2 copy-start.2
  581.5 1.1 copy-start.4
  581.5 1.2 copy-start.6
  582.2 1.3 copy-start.3
